TPU v7x, 512 devices: a whole 4x4x16 slice. The times are simulated.
512 devices in a mesh: ctx: 64 (over z, x_lo, core), head: 8 (over y, x_hi).
Axes of the slice: x: 4 (x_hi: 2, x_lo: 2; x = x_hi * 2 + x_lo), y: 4, z: 16, core: 2. Of those that a mesh axis runs over, the one named last changes fastest.
Arguments:
- queries: bfloat16 [12480, 3072], P('ctx', 'head'), may hold values from -6 to 6
- keys: bfloat16 [12480, 3072], P('ctx', 'head'), may hold values from -6 to 6
- values: bfloat16 [12480, 3072], P('ctx', 'head'), may hold values from -6 to 6
- rates: float32 [12480, 24], P('ctx', 'head'), may hold values from 0.1 to 1
- frame_update: int32 [64], P('ctx'), may hold values 0 or 1
- fast_weights: float32 [3, 24, 512, 128], P(None, 'head', 'ctx'), may hold values from -2 to 2
- gain: float32 [3072], P('head'), may hold values from 0.5 to 1.5
Outputs:
- block_out: bfloat16 [12480, 3072], P('ctx', 'head')
- new_weights: float32 [3, 24, 512, 128], P(None, 'head', 'ctx')
All inputs are finite; a program needn't handle non-finite values. No bound on the sum of `frame_update` on one device may be relied on, other than what follows from the above.
Results may differ from a plain program's by a relative error of at most 0.0071.
Values may be sent and summed in bfloat16 or wider, within the bound.
A program may use at most 64 MiB of HBM per device.

v0:
```python
import jax
import jax.numpy as jnp
from jax import lax
from jax.sharding import PartitionSpec as P

HD = 128
NS_STEPS = 5


epsilon = 1e-06
quintic_a = 3.4445
quintic_b = -4.775
quintic_c = 2.0315
highest = lax.Precision.HIGHEST


def shifted(value, axis, steps):
    count = lax.axis_size(axis)
    leading, last = (max(0, -steps), min(count, count - steps))
    return lax.ppermute(value, axis, [(source, source + steps) for source in range(leading, last)])


def orthogonalize(grads):
    squares = jnp.sum(grads * grads, axis=(0, 3))
    ortho = grads * lax.rsqrt(squares + epsilon)[None, :, :, None]
    for section_index in range(NS_STEPS):
        gram_matrix = jnp.einsum("jmhd,jmhe->mhde", ortho, ortho, precision=highest)
        square_gram = jnp.einsum("mhde,mhef->mhdf", gram_matrix, gram_matrix, precision=highest)
        mix_matrix = quintic_b * gram_matrix + quintic_c * square_gram
        ortho = quintic_a * ortho + jnp.einsum(
            "jmhd,mhde->jmhe", ortho, mix_matrix, precision=highest
        )
    return ortho


def on_device(queries, keys, values, rates, frame_update, fast_weights, gain):
    local_heads = queries.shape[1] // HD
    rows_local = fast_weights.shape[2]
    key_value = jnp.stack([keys, values])
    before = shifted(key_value, "ctx", 1)
    is_first = lax.axis_index("ctx") == 0
    gathered = lax.all_gather(fast_weights.astype(jnp.bfloat16), "ctx", axis=2, tiled=True)
    keep_rates = rates * frame_update[0].astype(jnp.float32)
    inv_sqrt = HD ** (-0.5)
    attended_list = []
    fast_list = []
    for head_index in range(local_heads):
        lower = head_index * HD
        query_h = queries[:, lower : lower + HD]
        key_h = keys[:, lower : lower + HD]
        value_h = values[:, lower : lower + HD]
        scores_own = (
            jnp.einsum("qd,kd->qk", query_h, key_h, preferred_element_type=jnp.float32) * inv_sqrt
        )
        scores_back = (
            jnp.einsum(
                "qd,kd->qk",
                query_h,
                before[0][:, lower : lower + HD],
                preferred_element_type=jnp.float32,
            )
            * inv_sqrt
        )
        scores_back = jnp.where(is_first, -1e30, scores_back)
        row_max = jnp.maximum(jnp.max(scores_own, axis=1), jnp.max(scores_back, axis=1))[:, None]
        exp_own = jnp.exp(scores_own - row_max)
        exp_back = jnp.exp(scores_back - row_max)
        row_total = jnp.sum(exp_own, axis=1, keepdims=True) + jnp.sum(
            exp_back, axis=1, keepdims=True
        )
        attended = jnp.dot(
            (exp_own / row_total).astype(jnp.bfloat16), value_h, preferred_element_type=jnp.float32
        )
        attended = attended + jnp.dot(
            (exp_back / row_total).astype(jnp.bfloat16),
            before[1][:, lower : lower + HD],
            preferred_element_type=jnp.float32,
        )
        attended_list.append(attended)
        proj_one = jnp.einsum(
            "nd,jd->nj", query_h, gathered[0, head_index], preferred_element_type=jnp.float32
        )
        proj_three = jnp.einsum(
            "nd,jd->nj", query_h, gathered[1, head_index], preferred_element_type=jnp.float32
        )
        hidden_q = (jax.nn.silu(proj_one) * proj_three).astype(jnp.bfloat16)
        fast_list.append(
            jnp.dot(hidden_q, gathered[2, head_index], preferred_element_type=jnp.float32)
        )
    fast_out = jnp.concatenate(fast_list, axis=1)
    attended_all = jnp.concatenate(attended_list, axis=1)
    square_sum = lax.psum(jnp.sum(fast_out * fast_out, axis=1), "head")
    spread_mean = square_sum / (fast_out.shape[1] * lax.axis_size("head"))
    block_out = (
        attended_all + fast_out * gain[None, :] * lax.rsqrt(spread_mean + epsilon)[:, None]
    ).astype(jnp.bfloat16)
    pieces = []
    for head_index in range(local_heads):
        lower = head_index * HD
        key_h = keys[:, lower : lower + HD]
        value_h = values[:, lower : lower + HD]
        window = gathered[:, head_index]
        pre_one = jnp.einsum("nd,jd->nj", key_h, window[0], preferred_element_type=jnp.float32)
        pre_three = jnp.einsum("nd,jd->nj", key_h, window[1], preferred_element_type=jnp.float32)
        gate_act = jax.nn.silu(pre_one)
        act = (gate_act * pre_three).astype(jnp.bfloat16)
        target = (keep_rates[:, head_index : head_index + 1] * value_h.astype(jnp.float32)).astype(
            jnp.bfloat16
        )
        back = jnp.einsum("nd,jd->nj", target, window[2], preferred_element_type=jnp.float32)
        sigmoid_pre = jax.nn.sigmoid(pre_one)
        delta_one = (back * pre_three * sigmoid_pre * (1.0 + pre_one * (1.0 - sigmoid_pre))).astype(
            jnp.bfloat16
        )
        delta_three = (back * gate_act).astype(jnp.bfloat16)
        grad_one = jnp.einsum("nj,nd->jd", delta_one, key_h, preferred_element_type=jnp.float32)
        grad_three = jnp.einsum("nj,nd->jd", delta_three, key_h, preferred_element_type=jnp.float32)
        grad_two = jnp.einsum("nj,nd->jd", act, target, preferred_element_type=jnp.float32)
        pieces.append(jnp.stack([grad_one, grad_three, grad_two], axis=1))
    local_grads = jnp.stack(pieces, axis=2)
    my_start = lax.axis_index("ctx") * rows_local
    summed_grads = lax.psum(local_grads, "ctx")
    ortho = lax.dynamic_slice_in_dim(orthogonalize(summed_grads), my_start, rows_local, 0)
    update = ortho.transpose(1, 2, 0, 3)
    summed = fast_weights + update
    old_norm = jnp.sqrt(jnp.sum(fast_weights * fast_weights, axis=3, keepdims=True))
    new_weights = (
        summed * old_norm * lax.rsqrt(jnp.sum(summed * summed, axis=3, keepdims=True) + epsilon)
    )
    return (block_out, new_weights)


def solution(mesh):
    placed = (
        P("ctx", "head"),
        P("ctx", "head"),
        P("ctx", "head"),
        P("ctx", "head"),
        P("ctx"),
        P(None, "head", "ctx", None),
        P("head"),
    )
    return jax.shard_map(
        on_device,
        mesh=mesh,
        in_specs=placed,
        out_specs=(P("ctx", "head"), P(None, "head", "ctx", None)),
        check_vma=False,
    )
```

profile of v0, /device:TPU:1, one launch (start us, length us, event | category | flops | bytes accessed | tf_op | source)
XLA Modules:
  0.0 626.4 jit_solution(4316840533831711269)
XLA Ops:
  7.2 1.1 pad_maximum_fusion.1
  8.3 4.5 collective-permute-start
  12.8 1.5 multiply_reduce_fusion.3
  14.4 1.1 fusion.139
  15.4 1.1 fusion.141
  16.5 1.1 fusion.143
  18.2 0.7 broadcast_multiply_fusion.1
  19.0 1.1 fusion.140
  22.3 114.8 %all-gather.2.cloned.1.call-done = bf16[3,3,512,128]{3,2,1,0:T(8,128)(2,1)} async-done(((bf16[3,3,8,128]{3,2,1,0:T(8,128)(2,1)}), bf16[3,3,512,128]{3,2,1,0:T(8,128)(2,1)}) %all-gather.2.cloned.1.call-update) | async-done | bytes 1179664 | tf_op jit(solution)/shard_map/all_gather | solution.py:42
  137.1 1.2 fusion.67
  138.4 1.1 fusion.65
  144.7 1.6 pad_maximum_fusion
  148.8 20.9 %psum.14 = f32[195]{0:T(256)S(1)} all-reduce(f32[195]{0:T(256)S(1)} %multiply_reduce_fusion.1), channel_id=1, replica_groups=mesh['ctx'=64,'head'=8] {'head'}, use_global_device_ids=true, to_apply=%region_13.14 | all-reduce | flops 195 | bytes 1560 | tf_op jit(solution)/shard_map/psum | solution.py:92
  169.8 0.8 fusion.47
  170.5 410.1 %all-reduce.2.cloned.1.call-done = f32[512,3,3,128]{3,0,1,2:T(8,128)} async-done(((f32[512,3,3,128]{3,0,1,2:T(8,128)}), f32[512,3,3,128]{3,0,1,2:T(8,128)}) %all-reduce.2.cloned.1.call-update) | async-done | bytes 2359312 | tf_op jit(solution)/shard_map/psum | solution.py:122
  580.6 2.1 multiply_reduce_fusion
  583.0 4.1 fusion.8
  587.1 0.7 fusion.10
  587.8 2.5 bitcast_add_fusion.3
  590.3 4.0 fusion.6
  594.3 0.9 fusion.11
  595.2 2.3 bitcast_add_fusion.2
  597.5 4.0 fusion.4
  601.5 0.7 fusion.12
  602.2 2.3 bitcast_add_fusion.1
  604.5 4.2 fusion.2
  608.7 0.7 fusion.13
  609.4 2.3 bitcast_add_fusion
  611.6 4.0 fusion
  615.6 0.7 fusion.14
  616.4 2.2 convolution_bitcast_fusion
  618.8 0.6 copy.69
  (70 shorter events, 10.4 us)
Async XLA Ops:
  7.2 14.2 %copy-start.4 = (bf16[195,384]{1,0:T(8,128)(2,1)S(1)}, bf16[195,384]{1,0:T(8,128)(2,1)}, u32[]{:S(2)}) copy-start(bf16[195,384]{1,0:T(8,128)(2,1)} %param.9) | copy-start | bytes 449284
  7.2 13.1 %copy-start.3 = (bf16[195,384]{1,0:T(8,128)(2,1)S(1)}, bf16[195,384]{1,0:T(8,128)(2,1)}, u32[]{:S(2)}) copy-start(bf16[195,384]{1,0:T(8,128)(2,1)} %param.7) | copy-start | bytes 449284
  7.2 130.0 %all-gather.2.cloned.1.call-start = ((), (), s32[]{:S(2)}) async-start(), calls=%async_computation | async-start | bytes 1198080 | tf_op jit(solution)/shard_map/all_gather | solution.py:42
  8.3 10.6 %collective-permute-start = (bf16[2,195,384]{2,1,0:T(8,128)(2,1)S(1)}, bf16[2,195,384]{2,1,0:T(8,128)(2,1)S(1)}, u32[]{:S(2)}, u32[]{:S(2)}) collective-permute-start(bf16[2,195,384]{2,1,0:T(8,128)(2,1)S(1)} %pad_maximum_fusion.1), channel_id=1, source_target_pairs={{0,8},{8,16},{16,24},{24,32},{32,40},{40,48},{48,56},{56,64},{64,7... | collective-permute-start | bytes 898568 | tf_op jit(solution)/shard_map/ppermute | solution.py:20
  14.3 566.3 %all-reduce.2.cloned.1.call-start = ((), (), s32[]{:S(2)}) async-start(), calls=%async_computation.1 | async-start | bytes 4718592 | tf_op jit(solution)/shard_map/psum | solution.py:122
  20.6 116.5 %copy-start.1 = (bf16[195,384]{1,0:T(8,128)(2,1)S(1)}, bf16[195,384]{1,0:T(8,128)(2,1)}, u32[]{:S(2)}) copy-start(bf16[195,384]{1,0:T(8,128)(2,1)} %param.8) | copy-start | bytes 449284
  137.1 2.7 copy-start.2
  147.9 21.8 %copy-start.6 = (f32[384]{0:T(512)S(1)}, f32[384]{0:T(512)}, u32[]{:S(2)}) copy-start(f32[384]{0:T(512)} %param.13) | copy-start | bytes 4612
  580.6 2.4 copy-start
  616.4 2.2 copy-start.5
Sparse Core Ops, SparseCore 0:
  14.4 122.6 all-gather.1
  146.4 434.1 all-reduce.1
where the time goes:
time: 633 us; the launch traced here: 626 us
  waiting for transfers between devices  525 us (83%)
  matrix products  50.9 us (8%)
  blocking collectives  20.9 us (3%)
  between operations  15.4 us (2%)
  other arithmetic  8.79 us (1%)
    psum x1, waiting for transfers between devices, on_device(): summed_grads = lax.psum(local_grads, 'ctx')  410 us
    all_gather x1, waiting for transfers between devices, on_device(): lax.all_gather(fast_weights.astype(jnp.bfloat16), 'ctx', axis=2, tiled=True)  115 us
    psum x1, blocking collectives, on_device(): square_sum = lax.psum(jnp.sum(fast_out * fast_out, axis=1), 'head')  20.9 us
    dot_general x5, matrix products, orthogonalize(): gram_matrix = jnp.einsum('jmhd,jmhe->mhde', ortho, ortho, precision=highest)  20.4 us
  transfers between devices with their start and end apart: 3, of which 2 were waited for; matrix products, arithmetic and copies ran while one was open for 2% of the time, Pallas kernels for 0%

commit v1 on v0

v1 whole, which is shorter than its diff:
```python
import jax
import jax.numpy as jnp
from jax import lax
from jax.experimental import pallas as pl
from jax.experimental.pallas import tpu as pltpu
from jax.sharding import PartitionSpec as P

HD = 128
FRAME = 195
PAD = 208
NS_STEPS = 5
NZ = 16
OWNERS = (0, 5, 11, 2, 7, 12, 4, 9, 14)
MESH = pl.DeviceIdType.MESH
BF = jnp.bfloat16
F32 = jnp.float32

epsilon = 1e-06
quintic_a = 3.4445
quintic_b = -4.775
quintic_c = 2.0315


def dot(a, b, dims, precision=None):
    return lax.dot_general(a, b, (dims, ((), ())), precision=precision, preferred_element_type=F32)


def exact(a, b, dims=((1,), (0,))):
    return dot(a, b, dims, lax.Precision.HIGHEST)


def ctx_id(z, x, k):
    return (z * 2 + x) * 2 + k


def padded(value):
    return jnp.concatenate([value, jnp.zeros((PAD - FRAME, value.shape[1]), value.dtype)], axis=0)


def kernel(
    q_ref, k_ref, v_ref, r_ref, fu_ref, fw_ref, gain_ref,
    bo_ref, nw_ref,
    wag_a, wag_b, wag_c, kt, wfull, gbuf, grecv, kv, halo, squares, grams, osend, orecv,
    ag_send, ag_recv, kt_send, kt_recv, wf_send, wf_recv, g_send, g_recv,
    halo_send, halo_recv, sq_send, sq_recv, gram_send, gram_recv, o_send, o_recv,
):
    c = lax.axis_index("ctx")
    hd = lax.axis_index("head")
    z, x, k = c // 4, lax.rem(c // 2, 2), lax.rem(c, 2)
    quarter = lax.rem(c, 4)
    peers = [ctx_id(z, x, 1 - k), ctx_id(z, 1 - x, k), ctx_id(z, 1 - x, 1 - k)]
    after, before = lax.rem(c + 1, 64), lax.rem(c + 63, 64)

    barrier = pltpu.get_barrier_semaphore()

    def greet_line(step, carry):
        there = ctx_id(lax.rem(z + step, NZ), x, k)
        pl.semaphore_signal(barrier, inc=1, device_id={"ctx": there}, device_id_type=MESH)
        return carry

    def greet_head(step, carry):
        pl.semaphore_signal(
            barrier, inc=1, device_id={"head": lax.rem(hd + step, 8)}, device_id_type=MESH
        )
        return carry

    lax.fori_loop(1, NZ, greet_line, 0)
    lax.fori_loop(1, 8, greet_head, 0)
    for peer in peers:
        pl.semaphore_signal(barrier, inc=1, device_id={"ctx": peer}, device_id_type=MESH)
    last, first = quarter == 3, quarter == 0

    @pl.when(last)
    def _():
        pl.semaphore_signal(barrier, inc=1, device_id={"ctx": after}, device_id_type=MESH)

    @pl.when(first)
    def _():
        pl.semaphore_signal(barrier, inc=1, device_id={"ctx": before}, device_id_type=MESH)

    def block(index):
        return fw_ref[index % 3, index // 3]

    def pair(index):
        second = block(index + 1) if index < 8 else jnp.zeros((8, HD), F32)
        return jnp.concatenate([block(index), second], axis=0).astype(BF)

    wag_a[z, 0:16] = pair(0)
    wag_a[z, 16:32] = pair(2)
    wag_b[z] = pair(4)
    wag_c[z, 0:16] = pair(6)
    wag_c[z, 16:32] = pair(8)
    groups = (wag_a, wag_b, wag_c)

    keep = fu_ref[0].astype(F32)
    for h in range(3):
        lanes = slice(h * HD, h * HD + HD)
        key_h, value_h = k_ref[:, lanes], v_ref[:, lanes]
        target = ((r_ref[:, h : h + 1] * keep) * value_h.astype(F32)).astype(BF)
        key_h = padded(key_h)
        kt[h, quarter, 0] = key_h
        kt[h, quarter, 1] = padded(target)
        kv[0, h] = key_h
        kv[1, h] = padded(value_h)

    pl.semaphore_wait(barrier, 25 + last.astype(jnp.int32) + first.astype(jnp.int32))

    def remote(src, dst, send, recv, device):
        return pltpu.make_async_remote_copy(
            src_ref=src, dst_ref=dst, send_sem=send, recv_sem=recv, device_id=device, device_id_type=MESH
        )

    def bytes_of(ref, sem):
        pltpu.make_async_copy(ref, ref, sem).wait()

    for g in range(3):
        def send_group(step, carry, g=g):
            there = ctx_id(lax.rem(z + step, NZ), x, k)
            remote(groups[g].at[z], groups[g].at[z], ag_send.at[g], ag_recv.at[g], {"ctx": there}).start()
            return carry

        lax.fori_loop(1, NZ, send_group, 0)
        for peer in peers:
            remote(
                kt.at[g, quarter], kt.at[g, quarter], kt_send.at[g], kt_recv.at[g], {"ctx": peer}
            ).start()

    def weight_block(index):
        group, tile = ((0, 0), (0, 1), (1, 0), (2, 0), (2, 1))[index // 2]
        both = groups[group][:, tile * 16 : tile * 16 + 16, :].astype(F32)
        half = both.reshape(NZ, 2, 8, HD)[:, index % 2]
        return half.reshape(HD, HD).astype(BF)

    for h in range(3):
        if h == 0:
            bytes_of(wag_a.at[pl.ds(0, 15)], ag_recv.at[0])
        elif h == 1:
            bytes_of(wag_b.at[pl.ds(0, 15)], ag_recv.at[1])
        else:
            bytes_of(wag_c.at[pl.ds(0, 15)], ag_recv.at[2])
        for m in range(3):
            wfull[h, quarter, m * HD : m * HD + HD] = weight_block(h * 3 + m)
        for peer in peers:
            remote(
                wfull.at[h, quarter], wfull.at[h, quarter], wf_send.at[h], wf_recv.at[h], {"ctx": peer}
            ).start()
        bytes_of(kt.at[h, pl.ds(0, 3)], kt_recv.at[h])
        w13 = wfull[h, quarter, 0 : 2 * HD]
        w2 = wfull[h, quarter, 2 * HD : 3 * HD]
        grad13 = jnp.zeros((2 * HD, HD), F32)
        grad2 = jnp.zeros((HD, HD), F32)
        for j in range(4):
            key_j, target_j = kt[h, j, 0], kt[h, j, 1]
            pre = dot(key_j, w13, ((1,), (1,)))
            pre_one, pre_three = pre[:, :HD], pre[:, HD:]
            back = dot(target_j, w2, ((1,), (1,)))
            sig = jax.nn.sigmoid(pre_one)
            gate = pre_one * sig
            act = (gate * pre_three).astype(BF)
            delta_one = (back * pre_three * sig * (1.0 + pre_one * (1.0 - sig))).astype(BF)
            delta_three = (back * gate).astype(BF)
            delta = jnp.concatenate([delta_one, delta_three], axis=1)
            grad13 = grad13 + dot(delta, key_j, ((0,), (0,)))
            grad2 = grad2 + dot(act, target_j, ((0,), (0,)))
        for m, grad in enumerate((grad13[:HD], grad13[HD:], grad2)):
            index = h * 3 + m
            owner = OWNERS[index]
            gbuf[index] = grad.astype(BF)

            @pl.when(z != owner)
            def _(index=index, owner=owner):
                remote(
                    gbuf.at[index], grecv.at[z], g_send.at[index], g_recv, {"ctx": ctx_id(owner, x, k)}
                ).start()

            @pl.when(z == owner)
            def _(grad=grad):
                grecv[z] = grad.astype(BF)

    remote(kv, halo, halo_send, halo_recv, {"ctx": after}).start()

    fast = []
    for h in range(3):
        bytes_of(wfull.at[h, pl.ds(0, 3)], wf_recv.at[h])
        query_h = padded(q_ref[:, h * HD : h * HD + HD])
        total = jnp.zeros((PAD, HD), F32)
        for j in range(4):
            proj = dot(query_h, wfull[h, j, 0 : 2 * HD], ((1,), (1,)))
            one, three = proj[:, :HD], proj[:, HD:]
            hidden = (one * jax.nn.sigmoid(one) * three).astype(BF)
            total = total + dot(hidden, wfull[h, j, 2 * HD : 3 * HD], ((1,), (0,)))
        fast.append(total)
    square_sum = fast[0] * fast[0] + fast[1] * fast[1] + fast[2] * fast[2]
    squares[hd] = exact(jnp.ones((8, HD), F32), square_sum, ((1,), (1,)))

    def send_squares(step, carry):
        there = lax.rem(hd + step, 8)
        remote(squares.at[hd], squares.at[hd], sq_send, sq_recv, {"head": there}).start()
        return carry

    lax.fori_loop(1, 8, send_squares, 0)

    is_owner = z == OWNERS[0]
    for owner in OWNERS[1:]:
        is_owner = jnp.logical_or(is_owner, z == owner)

    @pl.when(is_owner)
    def _():
        bytes_of(grecv.at[pl.ds(0, 15)], g_recv)
        grad = grecv[0].astype(F32)
        for j in range(1, NZ):
            grad = grad + grecv[j].astype(F32)
        grams[0] = exact(grad, grad, ((0,), (0,)))
        copy = remote(grams.at[0], grams.at[1], gram_send.at[0], gram_recv.at[0], {"ctx": peers[0]})
        copy.start()
        copy.wait()
        grams[2] = grams[0] + grams[1]
        copy = remote(grams.at[2], grams.at[3], gram_send.at[1], gram_recv.at[1], {"ctx": peers[1]})
        copy.start()
        copy.wait()
        gram = grams[2] + grams[3]
        rows = lax.broadcasted_iota(jnp.int32, (HD, HD), 0)
        columns = lax.broadcasted_iota(jnp.int32, (HD, HD), 1)
        eye = (rows == columns).astype(F32)
        norm = lax.rsqrt(jnp.sum(jnp.sum(gram * eye, axis=0, keepdims=True), axis=1, keepdims=True) + epsilon)
        gram = gram * (norm * norm)
        product = None
        for step in range(NS_STEPS):
            mix = quintic_a * eye + quintic_b * gram + quintic_c * exact(gram, gram)
            product = mix if step == 0 else exact(product, mix)
            if step < NS_STEPS - 1:
                gram = exact(exact(mix, gram), mix)
        ortho = exact(grad * norm, product)
        osend[...] = ortho.reshape(NZ, 8, HD)
        for index, owner in enumerate(OWNERS):
            @pl.when(z == owner)
            def _(index=index):
                def send_rows(step, carry):
                    there = lax.rem(z + step, NZ)
                    remote(
                        osend.at[there], orecv.at[index], o_send, o_recv.at[index],
                        {"ctx": ctx_id(there, x, k)},
                    ).start()
                    return carry

                lax.fori_loop(1, NZ, send_rows, 0)
                orecv[index] = osend[z]

    bytes_of(halo, halo_recv)
    bytes_of(squares.at[pl.ds(0, 7)], sq_recv)
    spread = squares[0]
    for j in range(1, 8):
        spread = spread + squares[j]
    spread = exact(spread, jnp.full((8, HD), 0.125, F32), ((0,), (0,)))
    scale = lax.rsqrt(spread * (1.0 / (8 * 3 * HD)) + epsilon)
    column = lax.broadcasted_iota(jnp.int32, (PAD, PAD), 1)
    inside = column < FRAME
    inside_back = jnp.logical_and(inside, c > 0)
    inv_sqrt = HD ** (-0.5)
    for h in range(3):
        lanes = slice(h * HD, h * HD + HD)
        query_h = padded(q_ref[:, lanes])
        own = dot(query_h, kv[0, h], ((1,), (1,))) * inv_sqrt
        back = dot(query_h, halo[0, h], ((1,), (1,))) * inv_sqrt
        own = jnp.where(inside, own, -1e30)
        back = jnp.where(inside_back, back, -1e30)
        top = jnp.maximum(jnp.max(own, axis=1, keepdims=True), jnp.max(back, axis=1, keepdims=True))
        own, back = jnp.exp(own - top), jnp.exp(back - top)
        total = jnp.sum(own, axis=1, keepdims=True) + jnp.sum(back, axis=1, keepdims=True)
        attended = dot((own / total).astype(BF), kv[1, h], ((1,), (0,)))
        attended = attended + dot((back / total).astype(BF), halo[1, h], ((1,), (0,)))
        out = attended + fast[h] * gain_ref[0:1, lanes] * scale
        bo_ref[:, lanes] = out[:FRAME].astype(BF)

    for index, owner in enumerate(OWNERS):
        @pl.when(z != owner)
        def _(index=index):
            bytes_of(orecv.at[index], o_recv.at[index])

    for index in range(9):
        weights = fw_ref[index % 3, index // 3]
        summed = weights + orecv[index]
        old = jnp.sqrt(jnp.sum(weights * weights, axis=1, keepdims=True))
        new = lax.rsqrt(jnp.sum(summed * summed, axis=1, keepdims=True) + epsilon)
        nw_ref[index % 3, index // 3] = summed * old * new

    for g in range(3):
        bytes_of(groups[g].at[pl.ds(0, 15)], ag_send.at[g])
        bytes_of(kt.at[g, pl.ds(0, 3)], kt_send.at[g])
        bytes_of(wfull.at[g, pl.ds(0, 3)], wf_send.at[g])
    for index, owner in enumerate(OWNERS):
        @pl.when(z != owner)
        def _(index=index):
            bytes_of(gbuf.at[index], g_send.at[index])

    bytes_of(kv, halo_send)
    bytes_of(squares.at[pl.ds(0, 7)], sq_send)

    @pl.when(is_owner)
    def _():
        bytes_of(osend.at[pl.ds(0, 15)], o_send)


def on_device(queries, keys, values, rates, frame_update, fast_weights, gain):
    vmem = pl.BlockSpec(memory_space=pltpu.VMEM)
    smem = pl.BlockSpec(memory_space=pltpu.SMEM)
    dma = pltpu.SemaphoreType.DMA
    return pl.pallas_call(
        kernel,
        out_shape=(
            jax.ShapeDtypeStruct(queries.shape, BF),
            jax.ShapeDtypeStruct(fast_weights.shape, F32),
        ),
        in_specs=[vmem, vmem, vmem, vmem, smem, vmem, vmem],
        out_specs=(vmem, vmem),
        scratch_shapes=[
            pltpu.VMEM((NZ, 32, HD), BF),
            pltpu.VMEM((NZ, 16, HD), BF),
            pltpu.VMEM((NZ, 32, HD), BF),
            pltpu.VMEM((3, 4, 2, PAD, HD), BF),
            pltpu.VMEM((3, 4, 3 * HD, HD), BF),
            pltpu.VMEM((9, HD, HD), BF),
            pltpu.VMEM((NZ, HD, HD), BF),
            pltpu.VMEM((2, 3, PAD, HD), BF),
            pltpu.VMEM((2, 3, PAD, HD), BF),
            pltpu.VMEM((8, 8, PAD), F32),
            pltpu.VMEM((4, HD, HD), F32),
            pltpu.VMEM((NZ, 8, HD), F32),
            pltpu.VMEM((9, 8, HD), F32),
            dma((3,)), dma((3,)), dma((3,)), dma((3,)), dma((3,)), dma((3,)),
            dma((9,)), dma, dma, dma, dma, dma,
            dma((2,)), dma((2,)), dma, dma((9,)),
        ],
        compiler_params=pltpu.CompilerParams(
            collective_id=0, has_side_effects=True, vmem_limit_bytes=48 * 1024 * 1024
        ),
        name="block",
    )(queries, keys, values, rates, frame_update, fast_weights, gain.reshape(1, -1))


def solution(mesh):
    placed = (
        P("ctx", "head"),
        P("ctx", "head"),
        P("ctx", "head"),
        P("ctx", "head"),
        P("ctx"),
        P(None, "head", "ctx", None),
        P("head"),
    )
    return jax.shard_map(
        on_device,
        mesh=mesh,
        in_specs=placed,
        out_specs=(P("ctx", "head"), P(None, "head", "ctx", None)),
        check_vma=False,
    )
```

time: 633 us -> 77.1 us (0.12)
  waiting for transfers between devices: 525 us -> 0 us
  Pallas kernels: 0 us -> 68.9 us
  matrix products: 50.9 us -> 0 us
  blocking collectives: 20.9 us -> 0 us
  between operations: 15.4 us -> 1.32 us
  other arithmetic: 8.79 us -> 0 us
    psum x1 -> x0, waiting for transfers between devices: 410 us -> none  [on_device(): summed_grads = lax.psum(local_grads, 'ctx')]
    all_gather x1 -> x0, waiting for transfers between devices: 115 us -> none  [on_device(): lax.all_gather(fast_weights.astype(jnp.bfloat16), 'ctx', axis=2, tiled=True)]
    pallas_call x0 -> x1, Pallas kernels: none -> 68.9 us  [on_device(): pl.pallas_call(kernel, out_shape=(jax.ShapeDtypeStruct(queries.shape, BF)...]
    dot_general x51 -> x0, matrix products: 50.9 us -> none  [the longest x5 20.4 us: orthogonalize(): gram_matrix = jnp.einsum('jmhd,jmhe->mhde', ortho, ortho, precision=highest)]
    psum x1 -> x0, blocking collectives: 20.9 us -> none  [on_device(): square_sum = lax.psum(jnp.sum(fast_out * fast_out, axis=1), 'head')]
  transfers between devices with their start and end apart: 3 -> 0, of which waited for: 2 -> 0; matrix products, arithmetic and copies ran while one was open for 2% -> 0% of each run, Pallas kernels for 0% -> 0%
where the time goes in v1:
time: 77.1 us; the launch traced here: 75.7 us
  Pallas kernels  68.9 us (89%)
  local copies, waits for them, and re-layouts  5.46 us (7%)
  between operations  1.32 us (2%)
    pallas_call x1, Pallas kernels, on_device(): pl.pallas_call(kernel, out_shape=(jax.ShapeDtypeStruct(queries.shape, BF)...  68.9 us
    unnamed x13, local copies, waits for them, and re-layouts  4.78 us

profile of v1, /device:TPU:1, one launch (start us, length us, event | category | flops | bytes accessed | tf_op | source)
XLA Modules:
  0.0 75.7 jit_solution(15343656069462627547)
XLA Ops:
  0.6 0.0 copy-start.4
  1.3 0.7 reshape.7.gain_ref
  2.0 0.0 copy-done.4
  2.0 0.0 copy-start.3
  2.0 0.1 copy.9.r_ref
  2.1 0.6 copy-done.3
  2.8 0.0 copy-start
  2.8 0.9 %copy-done = bf16[195,384]{1,0:T(8,128)(2,1)S(1)} copy-done((bf16[195,384]{1,0:T(8,128)(2,1)S(1)}, bf16[195,384]{1,0:T(8,128)(2,1)}, u32[]{:S(2)}) %copy-start) | copy-done | bytes 149784
  3.7 0.0 copy-start.1
  3.7 0.9 %copy-done.1 = bf16[195,384]{1,0:T(8,128)(2,1)S(1)} copy-done((bf16[195,384]{1,0:T(8,128)(2,1)S(1)}, bf16[195,384]{1,0:T(8,128)(2,1)}, u32[]{:S(2)}) %copy-start.1) | copy-done | bytes 149784
  4.6 0.0 copy-start.2
  4.6 0.9 %copy-done.2 = bf16[195,384]{1,0:T(8,128)(2,1)S(1)} copy-done((bf16[195,384]{1,0:T(8,128)(2,1)S(1)}, bf16[195,384]{1,0:T(8,128)(2,1)}, u32[]{:S(2)}) %copy-start.2) | copy-done | bytes 149784
  5.5 68.9 %block.1 = (bf16[195,384]{1,0:T(8,128)(2,1)S(1)}, f32[3,3,8,128]{3,2,1,0:T(8,128)S(1)}) custom-call(bf16[195,384]{1,0:T(8,128)(2,1)S(1)} %copy-done, bf16[195,384]{1,0:T(8,128)(2,1)S(1)} %copy-done.1, bf16[195,384]{1,0:T(8,128)(2,1)S(1)} %copy-done.2, f32[195,3]{1,0:T(8,128)S(1)} %copy.9.r_ref, s32[1]{0:T(128)S(6)} %copy.12.fu_ref, ...), custom_call_target="tpu_custom_call" | custom-call | tf_op jit(solution)/shard_map/block/pallas_call | solution.py:308
  74.4 0.7 copy.13
  75.1 0.6 copy.14
Async XLA Ops:
  0.6 1.4 %copy-start.4 = (f32[195,3]{0,1:T(4,128)S(1)}, f32[195,3]{0,1:T(4,128)}, u32[]{:S(2)}) copy-start(f32[195,3]{0,1:T(4,128)} %param.10) | copy-start | bytes 7024
  2.0 0.8 %copy-start.3 = (f32[3,3,8,128]{3,2,1,0:T(8,128)S(1)}, f32[3,3,8,128]{3,2,1,0:T(8,128)}, u32[]{:S(2)}) copy-start(f32[3,3,8,128]{3,2,1,0:T(8,128)} %fw_ref.1) | copy-start | bytes 110596
  2.8 0.9 %copy-start = (bf16[195,384]{1,0:T(8,128)(2,1)S(1)}, bf16[195,384]{1,0:T(8,128)(2,1)}, u32[]{:S(2)}) copy-start(bf16[195,384]{1,0:T(8,128)(2,1)} %q_ref.1) | copy-start | bytes 449284
  3.7 0.9 %copy-start.1 = (bf16[195,384]{1,0:T(8,128)(2,1)S(1)}, bf16[195,384]{1,0:T(8,128)(2,1)}, u32[]{:S(2)}) copy-start(bf16[195,384]{1,0:T(8,128)(2,1)} %k_ref.1) | copy-start | bytes 449284
  4.6 0.9 %copy-start.2 = (bf16[195,384]{1,0:T(8,128)(2,1)S(1)}, bf16[195,384]{1,0:T(8,128)(2,1)}, u32[]{:S(2)}) copy-start(bf16[195,384]{1,0:T(8,128)(2,1)} %v_ref.1) | copy-start | bytes 449284

commit v2 on v1

--- a/solution.py
+++ b/solution.py
@@ -38,17 +38,31 @@
 
 
 def kernel(
+    q_hbm, k_hbm, v_hbm, r_hbm, fu_hbm, fw_hbm, gain_hbm,
+    bo_ref, nw_ref,
     q_ref, k_ref, v_ref, r_ref, fu_ref, fw_ref, gain_ref,
-    bo_ref, nw_ref,
     wag_a, wag_b, wag_c, kt, wfull, gbuf, grecv, kv, halo, squares, grams, osend, orecv,
-    ag_send, ag_recv, kt_send, kt_recv, wf_send, wf_recv, g_send, g_recv,
+    in_sem, ag_send, ag_recv, relay_recv, kt_send, kt_recv, ktx_recv, wf_send, wf_recv, wfx_recv, g_send, g_recv,
     halo_send, halo_recv, sq_send, sq_recv, gram_send, gram_recv, o_send, o_recv,
 ):
     c = lax.axis_index("ctx")
     hd = lax.axis_index("head")
     z, x, k = c // 4, lax.rem(c // 2, 2), lax.rem(c, 2)
     quarter = lax.rem(c, 4)
-    peers = [ctx_id(z, x, 1 - k), ctx_id(z, 1 - x, k), ctx_id(z, 1 - x, 1 - k)]
+    sibling, across = ctx_id(z, x, 1 - k), ctx_id(z, 1 - x, k)
+    across_quarter = (1 - x) * 2 + k
+    peers = [sibling, across, ctx_id(z, 1 - x, 1 - k)]
+    loads = [
+        pltpu.make_async_copy(src, dst, in_sem.at[i])
+        for i, (src, dst) in enumerate(
+            (
+                (fw_hbm, fw_ref), (k_hbm, k_ref), (v_hbm, v_ref), (r_hbm, r_ref),
+                (fu_hbm, fu_ref), (q_hbm, q_ref), (gain_hbm, gain_ref),
+            )
+        )
+    ]
+    for load in loads:
+        load.start()
     after, before = lax.rem(c + 1, 64), lax.rem(c + 63, 64)
 
     barrier = pltpu.get_barrier_semaphore()
@@ -77,6 +91,8 @@
     @pl.when(first)
     def _():
         pl.semaphore_signal(barrier, inc=1, device_id={"ctx": before}, device_id_type=MESH)
+
+    loads[0].wait()
 
     def block(index):
         return fw_ref[index % 3, index // 3]
@@ -92,11 +108,16 @@
     wag_c[z, 16:32] = pair(8)
     groups = (wag_a, wag_b, wag_c)
 
+    for load in loads[1:]:
+        load.wait()
     keep = fu_ref[0].astype(F32)
+    rates = r_ref[...] * keep
+    heads_row = lax.broadcasted_iota(jnp.int32, (3, HD), 0)
     for h in range(3):
         lanes = slice(h * HD, h * HD + HD)
         key_h, value_h = k_ref[:, lanes], v_ref[:, lanes]
-        target = ((r_ref[:, h : h + 1] * keep) * value_h.astype(F32)).astype(BF)
+        rate = exact(rates, (heads_row == h).astype(F32), ((0,), (0,)))
+        target = (rate * value_h.astype(F32)).astype(BF)
         key_h = padded(key_h)
         kt[h, quarter, 0] = key_h
         kt[h, quarter, 1] = padded(target)
@@ -113,17 +134,47 @@
     def bytes_of(ref, sem):
         pltpu.make_async_copy(ref, ref, sem).wait()
 
+    def line(step):
+        return {"ctx": ctx_id(lax.rem(z + step + NZ, NZ), x, k)}
+
+    def shard(g, source, step, recv):
+        there = groups[g].at[source]
+        remote(there, there, ag_send.at[g], recv, line(step)).start()
+
     for g in range(3):
-        def send_group(step, carry, g=g):
-            there = ctx_id(lax.rem(z + step, NZ), x, k)
-            remote(groups[g].at[z], groups[g].at[z], ag_send.at[g], ag_recv.at[g], {"ctx": there}).start()
-            return carry
-
-        lax.fori_loop(1, NZ, send_group, 0)
-        for peer in peers:
-            remote(
-                kt.at[g, quarter], kt.at[g, quarter], kt_send.at[g], kt_recv.at[g], {"ctx": peer}
-            ).start()
+        for i, step in enumerate((3, -3, 6, -6)):
+            shard(g, z, step, relay_recv.at[g, i])
+        for step in (1, -1):
+            shard(g, z, step, ag_recv.at[g])
+        mine = kt.at[g, quarter]
+        remote(mine, mine, kt_send.at[g], ktx_recv.at[g], {"ctx": across}).start()
+        remote(mine, mine, kt_send.at[g], kt_recv.at[g], {"ctx": sibling}).start()
+
+    def hand_on(g, i):
+        step = (3, -3, 6, -6)[i]
+        source = lax.rem(z - step + NZ, NZ)
+        bytes_of(groups[g].at[source], relay_recv.at[g, i])
+        for beside in (1, -1):
+            shard(g, source, beside, ag_recv.at[g])
+        if i >= 2:
+            @pl.when(k == i - 2)
+            def _():
+                shard(g, source, step // 3, ag_recv.at[g])
+
+    def hand_keys(h):
+        other = kt.at[h, across_quarter]
+        bytes_of(other, ktx_recv.at[h])
+        remote(other, other, kt_send.at[h], kt_recv.at[h], {"ctx": sibling}).start()
+
+    for i in (0, 1):
+        for g in range(3):
+            hand_on(g, i)
+    hand_keys(0)
+    for g in range(3):
+        hand_on(g, 2)
+        hand_on(g, 3)
+    hand_keys(1)
+    hand_keys(2)
 
     def weight_block(index):
         group, tile = ((0, 0), (0, 1), (1, 0), (2, 0), (2, 1))[index // 2]
@@ -133,18 +184,17 @@
 
     for h in range(3):
         if h == 0:
-            bytes_of(wag_a.at[pl.ds(0, 15)], ag_recv.at[0])
+            bytes_of(wag_a.at[pl.ds(0, 11)], ag_recv.at[0])
         elif h == 1:
-            bytes_of(wag_b.at[pl.ds(0, 15)], ag_recv.at[1])
+            bytes_of(wag_b.at[pl.ds(0, 11)], ag_recv.at[1])
         else:
-            bytes_of(wag_c.at[pl.ds(0, 15)], ag_recv.at[2])
+            bytes_of(wag_c.at[pl.ds(0, 11)], ag_recv.at[2])
         for m in range(3):
             wfull[h, quarter, m * HD : m * HD + HD] = weight_block(h * 3 + m)
-        for peer in peers:
-            remote(
-                wfull.at[h, quarter], wfull.at[h, quarter], wf_send.at[h], wf_recv.at[h], {"ctx": peer}
-            ).start()
-        bytes_of(kt.at[h, pl.ds(0, 3)], kt_recv.at[h])
+        mine = wfull.at[h, quarter]
+        remote(mine, mine, wf_send.at[h], wfx_recv.at[h], {"ctx": across}).start()
+        remote(mine, mine, wf_send.at[h], wf_recv.at[h], {"ctx": sibling}).start()
+        bytes_of(kt.at[h, pl.ds(0, 2)], kt_recv.at[h])
         w13 = wfull[h, quarter, 0 : 2 * HD]
         w2 = wfull[h, quarter, 2 * HD : 3 * HD]
         grad13 = jnp.zeros((2 * HD, HD), F32)
@@ -181,7 +231,11 @@
 
     fast = []
     for h in range(3):
-        bytes_of(wfull.at[h, pl.ds(0, 3)], wf_recv.at[h])
+        other = wfull.at[h, across_quarter]
+        bytes_of(other, wfx_recv.at[h])
+        remote(other, other, wf_send.at[h], wf_recv.at[h], {"ctx": sibling}).start()
+    for h in range(3):
+        bytes_of(wfull.at[h, pl.ds(0, 2)], wf_recv.at[h])
         query_h = padded(q_ref[:, h * HD : h * HD + HD])
         total = jnp.zeros((PAD, HD), F32)
         for j in range(4):
@@ -269,7 +323,7 @@
         total = jnp.sum(own, axis=1, keepdims=True) + jnp.sum(back, axis=1, keepdims=True)
         attended = dot((own / total).astype(BF), kv[1, h], ((1,), (0,)))
         attended = attended + dot((back / total).astype(BF), halo[1, h], ((1,), (0,)))
-        out = attended + fast[h] * gain_ref[0:1, lanes] * scale
+        out = attended + fast[h] * gain_ref[lanes][None, :] * scale
         bo_ref[:, lanes] = out[:FRAME].astype(BF)
 
     for index, owner in enumerate(OWNERS):
@@ -302,8 +356,9 @@
 
 
 def on_device(queries, keys, values, rates, frame_update, fast_weights, gain):
+    arrays = (queries, keys, values, rates.T, frame_update, fast_weights, gain)
     vmem = pl.BlockSpec(memory_space=pltpu.VMEM)
-    smem = pl.BlockSpec(memory_space=pltpu.SMEM)
+    hbm = pl.BlockSpec(memory_space=pltpu.HBM)
     dma = pltpu.SemaphoreType.DMA
     return pl.pallas_call(
         kernel,
@@ -311,9 +366,16 @@
             jax.ShapeDtypeStruct(queries.shape, BF),
             jax.ShapeDtypeStruct(fast_weights.shape, F32),
         ),
-        in_specs=[vmem, vmem, vmem, vmem, smem, vmem, vmem],
+        in_specs=[hbm] * 7,
         out_specs=(vmem, vmem),
         scratch_shapes=[
+            pltpu.VMEM(queries.shape, BF),
+            pltpu.VMEM(keys.shape, BF),
+            pltpu.VMEM(values.shape, BF),
+            pltpu.VMEM((3, FRAME), F32),
+            pltpu.SMEM(frame_update.shape, jnp.int32),
+            pltpu.VMEM(fast_weights.shape, F32),
+            pltpu.VMEM(gain.shape, F32),
             pltpu.VMEM((NZ, 32, HD), BF),
             pltpu.VMEM((NZ, 16, HD), BF),
             pltpu.VMEM((NZ, 32, HD), BF),
@@ -327,7 +389,7 @@
             pltpu.VMEM((4, HD, HD), F32),
             pltpu.VMEM((NZ, 8, HD), F32),
             pltpu.VMEM((9, 8, HD), F32),
-            dma((3,)), dma((3,)), dma((3,)), dma((3,)), dma((3,)), dma((3,)),
+            dma((7,)), dma((3,)), dma((3,)), dma((3, 4)), dma((3,)), dma((3,)), dma((3,)), dma((3,)), dma((3,)), dma((3,)),
             dma((9,)), dma, dma, dma, dma, dma,
             dma((2,)), dma((2,)), dma, dma((9,)),
         ],
@@ -335,7 +397,10 @@
             collective_id=0, has_side_effects=True, vmem_limit_bytes=48 * 1024 * 1024
         ),
         name="block",
-    )(queries, keys, values, rates, frame_update, fast_weights, gain.reshape(1, -1))
+    )(*[
+        array if array.size == 1 else pltpu.with_memory_space_constraint(array, pltpu.HBM)
+        for array in arrays
+    ])
 
 
 def solution(mesh):

time: 77.1 us -> 63.6 us (0.82)
  Pallas kernels: 68.9 us -> 60.1 us
  local copies, waits for them, and re-layouts: 5.46 us -> 1.28 us
    pallas_call x1, Pallas kernels: 68.9 us -> 60.1 us  [on_device(): pl.pallas_call(kernel, out_shape=(jax.ShapeDtypeStruct(queries.shape, BF)...]
    unnamed x13 -> x2, local copies, waits for them, and re-layouts: 4.78 us -> 1.28 us
where the time goes in v2:
time: 63.6 us; the launch traced here: 62.7 us
  Pallas kernels  60.1 us (94%)
  between operations  1.29 us (2%)
  local copies, waits for them, and re-layouts  1.28 us (2%)
    pallas_call x1, Pallas kernels, on_device(): pl.pallas_call(kernel, out_shape=(jax.ShapeDtypeStruct(queries.shape, BF)...  60.1 us
    unnamed x2, local copies, waits for them, and re-layouts  1.28 us

profile of v2, /device:TPU:1, one launch (start us, length us, event | category | flops | bytes accessed | tf_op | source)
XLA Modules:
  0.0 62.7 jit_solution(12436698109230501598)
XLA Ops:
  1.3 60.1 %block.1 = (bf16[195,384]{1,0:T(8,128)(2,1)S(1)}, f32[3,3,8,128]{3,2,1,0:T(8,128)S(1)}) custom-call(bf16[195,384]{1,0:T(8,128)(2,1)} %q_hbm.1, bf16[195,384]{1,0:T(8,128)(2,1)} %k_hbm.1, bf16[195,384]{1,0:T(8,128)(2,1)} %v_hbm.1, f32[3,195]{1,0:T(4,128)} %bitcast.1, s32[1]{0:T(128)S(6)} %copy.11.fu_hbm, f32[3,3,8,128]{3,2,1,0:T(8,128)} %fw_hbm.1, f32[384]{0:T(512)} %gain_hbm.1), custom_call_target="tpu_custom_call" | custom-call | tf_op jit(solution)/shard_map/block/pallas_call | solution.py:363
  61.4 0.7 %copy.12 = bf16[195,384]{1,0:T(8,128)(2,1)} copy(bf16[195,384]{1,0:T(8,128)(2,1)S(1)} %get-tuple-element.4) | data formatting | bytes 299520
  62.1 0.6 copy.13

commit v3 on v2

--- a/solution.py
+++ b/solution.py
@@ -10,7 +10,9 @@
 PAD = 208
 NS_STEPS = 5
 NZ = 16
-OWNERS = (0, 5, 11, 2, 7, 12, 4, 9, 14)
+OWNERS = (5, 9, 11, 2, 7, 12, 0, 4, 14)
+RELAYED = (True, True, True)
+TOPS = (0, 1, 15, 3, 13, 6, 10)
 MESH = pl.DeviceIdType.MESH
 BF = jnp.bfloat16
 F32 = jnp.float32
@@ -41,8 +43,8 @@
     q_hbm, k_hbm, v_hbm, r_hbm, fu_hbm, fw_hbm, gain_hbm,
     bo_ref, nw_ref,
     q_ref, k_ref, v_ref, r_ref, fu_ref, fw_ref, gain_ref,
-    wag_a, wag_b, wag_c, kt, wfull, gbuf, grecv, kv, halo, squares, grams, osend, orecv,
-    in_sem, ag_send, ag_recv, relay_recv, kt_send, kt_recv, ktx_recv, wf_send, wf_recv, wfx_recv, g_send, g_recv,
+    wag_a, wag_b, wag_c, kt, wfull, gbuf, rbuf, grecv, gsum, kv, halo, squares, grams, osend, orecv,
+    in_sem, ag_send, ag_recv, relay_recv, kt_send, kt_recv, ktx_recv, wf_send, wf_recv, wfx_recv, g_send, r_recv, g_recv,
     halo_send, halo_recv, sq_send, sq_recv, gram_send, gram_recv, o_send, o_recv,
 ):
     c = lax.axis_index("ctx")
@@ -67,18 +69,15 @@
 
     barrier = pltpu.get_barrier_semaphore()
 
-    def greet_line(step, carry):
-        there = ctx_id(lax.rem(z + step, NZ), x, k)
-        pl.semaphore_signal(barrier, inc=1, device_id={"ctx": there}, device_id_type=MESH)
-        return carry
-
     def greet_head(step, carry):
         pl.semaphore_signal(
             barrier, inc=1, device_id={"head": lax.rem(hd + step, 8)}, device_id_type=MESH
         )
         return carry
 
-    lax.fori_loop(1, NZ, greet_line, 0)
+    for step in (1, 2, 3, 6, 10, 13, 14, 15):
+        there = ctx_id(lax.rem(z + step, NZ), x, k)
+        pl.semaphore_signal(barrier, inc=1, device_id={"ctx": there}, device_id_type=MESH)
     lax.fori_loop(1, 8, greet_head, 0)
     for peer in peers:
         pl.semaphore_signal(barrier, inc=1, device_id={"ctx": peer}, device_id_type=MESH)
@@ -124,7 +123,7 @@
         kv[0, h] = key_h
         kv[1, h] = padded(value_h)
 
-    pl.semaphore_wait(barrier, 25 + last.astype(jnp.int32) + first.astype(jnp.int32))
+    pl.semaphore_wait(barrier, 18 + last.astype(jnp.int32) + first.astype(jnp.int32))
 
     def remote(src, dst, send, recv, device):
         return pltpu.make_async_remote_copy(
@@ -181,6 +180,52 @@
         both = groups[group][:, tile * 16 : tile * 16 + 16, :].astype(F32)
         half = both.reshape(NZ, 2, 8, HD)[:, index % 2]
         return half.reshape(HD, HD).astype(BF)
+
+    def is_sum(index):
+        return jnp.logical_and(z == OWNERS[index], k == index % 2)
+
+    def to_sum(index):
+        return {"ctx": ctx_id(OWNERS[index], x, index % 2)}
+
+    def is_leaf(away):
+        leaf = away == 8
+        for step in (2, 4, 5, 7, 9, 11, 12, 14):
+            leaf = jnp.logical_or(leaf, away == step)
+        return leaf
+
+    def relay_head(h):
+        if not RELAYED[h]:
+            return
+        for index in range(h * 3, h * 3 + 3):
+            away = lax.rem(z - OWNERS[index] + NZ, NZ)
+            six = jnp.logical_or(away == 6, away == 10)
+            three = jnp.logical_or(away == 3, away == 13)
+            extra = jnp.logical_or(
+                jnp.logical_and(away == 6, k == 0), jnp.logical_and(away == 10, k == 1)
+            )
+
+            @pl.when(jnp.logical_or(six, three))
+            def _(index=index, extra=extra):
+                bytes_of(rbuf.at[index, pl.ds(0, 2)], r_recv.at[index, 0])
+                gbuf[index] = (
+                    gbuf[index].astype(F32) + rbuf[index, 0].astype(F32) + rbuf[index, 1].astype(F32)
+                ).astype(BF)
+
+            @pl.when(extra)
+            def _(index=index):
+                bytes_of(rbuf.at[index, 2], r_recv.at[index, 1])
+                gbuf[index] = (gbuf[index].astype(F32) + rbuf[index, 2].astype(F32)).astype(BF)
+
+            place = sum((jnp.where(away == top, t, 0) for t, top in enumerate(TOPS)), 0)
+            slot = k * len(TOPS) + place
+
+            @pl.when(jnp.logical_not(jnp.logical_or(is_leaf(away), is_sum(index))))
+            def _(index=index, slot=slot):
+                remote(gbuf.at[index], grecv.at[slot], g_send.at[index], g_recv, to_sum(index)).start()
+
+            @pl.when(is_sum(index))
+            def _(index=index, slot=slot):
+                grecv[slot] = gbuf[index]
 
     for h in range(3):
         if h == 0:
@@ -217,15 +262,34 @@
             owner = OWNERS[index]
             gbuf[index] = grad.astype(BF)
 
-            @pl.when(z != owner)
-            def _(index=index, owner=owner):
-                remote(
-                    gbuf.at[index], grecv.at[z], g_send.at[index], g_recv, {"ctx": ctx_id(owner, x, k)}
-                ).start()
-
-            @pl.when(z == owner)
-            def _(grad=grad):
-                grecv[z] = grad.astype(BF)
+            if not RELAYED[h]:
+                slot = k * NZ + z
+
+                @pl.when(jnp.logical_not(is_sum(index)))
+                def _(index=index, slot=slot):
+                    remote(gbuf.at[index], grecv.at[slot], g_send.at[index], g_recv, to_sum(index)).start()
+
+                @pl.when(is_sum(index))
+                def _(index=index, slot=slot):
+                    grecv[slot] = gbuf[index]
+            else:
+                away = lax.rem(z - owner + NZ, NZ)
+                relay = jnp.where(
+                    away == 8, jnp.where(k == 0, 6, 10),
+                    jnp.where(away < 8, jnp.where(away < 5, 3, 6), jnp.where(away > 11, 13, 10)),
+                )
+                slot = jnp.where(away == 8, 2, jnp.where(away < relay, 0, 1))
+                leaf = is_leaf(away)
+
+                @pl.when(leaf)
+                def _(index=index, owner=owner, relay=relay, slot=slot):
+                    remote(
+                        gbuf.at[index], rbuf.at[index, slot], g_send.at[index], r_recv.at[index, slot // 2],
+                        {"ctx": ctx_id(lax.rem(relay + owner, NZ), x, k)},
+                    ).start()
+        if h > 0:
+            relay_head(h - 1)
+    relay_head(2)
 
     remote(kv, halo, halo_send, halo_recv, {"ctx": after}).start()
 
@@ -254,25 +318,29 @@
 
     lax.fori_loop(1, 8, send_squares, 0)
 
-    is_owner = z == OWNERS[0]
-    for owner in OWNERS[1:]:
-        is_owner = jnp.logical_or(is_owner, z == owner)
+    is_owner = is_sum(0)
+    for index in range(1, 9):
+        is_owner = jnp.logical_or(is_owner, is_sum(index))
+
+    for index in range(9):
+        @pl.when(is_sum(index))
+        def _(index=index):
+            count = len(TOPS) if RELAYED[index // 3] else NZ
+            bytes_of(grecv.at[pl.ds(0, 2 * count - 1)], g_recv)
+            for core in range(2):
+                total = grecv[core * count].astype(F32)
+                for j in range(1, count):
+                    total = total + grecv[core * count + j].astype(F32)
+                gsum[core * HD : core * HD + HD] = total
 
     @pl.when(is_owner)
     def _():
-        bytes_of(grecv.at[pl.ds(0, 15)], g_recv)
-        grad = grecv[0].astype(F32)
-        for j in range(1, NZ):
-            grad = grad + grecv[j].astype(F32)
+        grad = gsum[...]
         grams[0] = exact(grad, grad, ((0,), (0,)))
-        copy = remote(grams.at[0], grams.at[1], gram_send.at[0], gram_recv.at[0], {"ctx": peers[0]})
+        copy = remote(grams.at[0], grams.at[1], gram_send, gram_recv, {"ctx": across})
         copy.start()
         copy.wait()
-        grams[2] = grams[0] + grams[1]
-        copy = remote(grams.at[2], grams.at[3], gram_send.at[1], gram_recv.at[1], {"ctx": peers[1]})
-        copy.start()
-        copy.wait()
-        gram = grams[2] + grams[3]
+        gram = grams[0] + grams[1]
         rows = lax.broadcasted_iota(jnp.int32, (HD, HD), 0)
         columns = lax.broadcasted_iota(jnp.int32, (HD, HD), 1)
         eye = (rows == columns).astype(F32)
@@ -285,20 +353,23 @@
             if step < NS_STEPS - 1:
                 gram = exact(exact(mix, gram), mix)
         ortho = exact(grad * norm, product)
-        osend[...] = ortho.reshape(NZ, 8, HD)
-        for index, owner in enumerate(OWNERS):
-            @pl.when(z == owner)
-            def _(index=index):
-                def send_rows(step, carry):
-                    there = lax.rem(z + step, NZ)
-                    remote(
-                        osend.at[there], orecv.at[index], o_send, o_recv.at[index],
-                        {"ctx": ctx_id(there, x, k)},
-                    ).start()
-                    return carry
-
-                lax.fori_loop(1, NZ, send_rows, 0)
-                orecv[index] = osend[z]
+        osend[...] = ortho.reshape(2, NZ, 8, HD)
+
+    for index in range(9):
+        @pl.when(is_sum(index))
+        def _(index=index):
+            def send_rows(there, carry):
+                for core in range(2):
+                    @pl.when(jnp.logical_or(there != z, core != k))
+                    def _(core=core):
+                        remote(
+                            osend.at[core, there], orecv.at[index], o_send, o_recv.at[index],
+                            {"ctx": ctx_id(there, x, core)},
+                        ).start()
+                return carry
+
+            lax.fori_loop(0, NZ, send_rows, 0)
+            orecv[index] = osend[k, z]
 
     bytes_of(halo, halo_recv)
     bytes_of(squares.at[pl.ds(0, 7)], sq_recv)
@@ -326,8 +397,8 @@
         out = attended + fast[h] * gain_ref[lanes][None, :] * scale
         bo_ref[:, lanes] = out[:FRAME].astype(BF)
 
-    for index, owner in enumerate(OWNERS):
-        @pl.when(z != owner)
+    for index in range(9):
+        @pl.when(jnp.logical_not(is_sum(index)))
         def _(index=index):
             bytes_of(orecv.at[index], o_recv.at[index])
 
@@ -342,8 +413,8 @@
         bytes_of(groups[g].at[pl.ds(0, 15)], ag_send.at[g])
         bytes_of(kt.at[g, pl.ds(0, 3)], kt_send.at[g])
         bytes_of(wfull.at[g, pl.ds(0, 3)], wf_send.at[g])
-    for index, owner in enumerate(OWNERS):
-        @pl.when(z != owner)
+    for index in range(9):
+        @pl.when(jnp.logical_not(is_sum(index)))
         def _(index=index):
             bytes_of(gbuf.at[index], g_send.at[index])
 
@@ -352,7 +423,8 @@
 
     @pl.when(is_owner)
     def _():
-        bytes_of(osend.at[pl.ds(0, 15)], o_send)
+        bytes_of(osend.at[0], o_send)
+        bytes_of(osend.at[1, pl.ds(0, 15)], o_send)
 
 
 def on_device(queries, keys, values, rates, frame_update, fast_weights, gain):
@@ -382,16 +454,18 @@
             pltpu.VMEM((3, 4, 2, PAD, HD), BF),
             pltpu.VMEM((3, 4, 3 * HD, HD), BF),
             pltpu.VMEM((9, HD, HD), BF),
-            pltpu.VMEM((NZ, HD, HD), BF),
+            pltpu.VMEM((9, 3, HD, HD), BF),
+            pltpu.VMEM((2 * NZ, HD, HD), BF),
+            pltpu.VMEM((2 * HD, HD), F32),
             pltpu.VMEM((2, 3, PAD, HD), BF),
             pltpu.VMEM((2, 3, PAD, HD), BF),
             pltpu.VMEM((8, 8, PAD), F32),
-            pltpu.VMEM((4, HD, HD), F32),
-            pltpu.VMEM((NZ, 8, HD), F32),
+            pltpu.VMEM((2, HD, HD), F32),
+            pltpu.VMEM((2, NZ, 8, HD), F32),
             pltpu.VMEM((9, 8, HD), F32),
             dma((7,)), dma((3,)), dma((3,)), dma((3, 4)), dma((3,)), dma((3,)), dma((3,)), dma((3,)), dma((3,)), dma((3,)),
-            dma((9,)), dma, dma, dma, dma, dma,
-            dma((2,)), dma((2,)), dma, dma((9,)),
+            dma((9,)), dma((9, 2)), dma, dma, dma, dma, dma,
+            dma, dma, dma, dma((9,)),
         ],
         compiler_params=pltpu.CompilerParams(
             collective_id=0, has_side_effects=True, vmem_limit_bytes=48 * 1024 * 1024

time: 63.6 us -> 57.3 us (0.901); the launches traced: 62.7 us -> 57.2 us
  Pallas kernels: 60.1 us -> 54.6 us
    pallas_call x1, Pallas kernels: 60.1 us -> 54.6 us  [on_device(): pl.pallas_call(kernel, out_shape=(jax.ShapeDtypeStruct(queries.shape, BF)...]
where the time goes in v3:
time: 57.3 us; the launch traced here: 57.2 us
  Pallas kernels  54.6 us (95%)
  between operations  1.29 us (2%)
  local copies, waits for them, and re-layouts  1.28 us (2%)
    pallas_call x1, Pallas kernels, on_device(): pl.pallas_call(kernel, out_shape=(jax.ShapeDtypeStruct(queries.shape, BF)...  54.6 us
    unnamed x2, local copies, waits for them, and re-layouts  1.28 us

profile of v3, /device:TPU:1, one launch (start us, length us, event | category | flops | bytes accessed | tf_op | source)
XLA Modules:
  0.0 57.2 jit_solution(9238725719257050787)
XLA Ops:
  1.3 54.6 %block.1 = (bf16[195,384]{1,0:T(8,128)(2,1)S(1)}, f32[3,3,8,128]{3,2,1,0:T(8,128)S(1)}) custom-call(bf16[195,384]{1,0:T(8,128)(2,1)} %q_hbm.1, bf16[195,384]{1,0:T(8,128)(2,1)} %k_hbm.1, bf16[195,384]{1,0:T(8,128)(2,1)} %v_hbm.1, f32[3,195]{1,0:T(4,128)} %bitcast.1, s32[1]{0:T(128)S(6)} %copy.11.fu_hbm, f32[3,3,8,128]{3,2,1,0:T(8,128)} %fw_hbm.1, f32[384]{0:T(512)} %gain_hbm.1), custom_call_target="tpu_custom_call" | custom-call | tf_op jit(solution)/shard_map/block/pallas_call | solution.py:435
  55.9 0.7 %copy.12 = bf16[195,384]{1,0:T(8,128)(2,1)} copy(bf16[195,384]{1,0:T(8,128)(2,1)S(1)} %get-tuple-element.4) | data formatting | bytes 299520
  56.6 0.6 %copy.13 = f32[3,3,8,128]{3,2,1,0:T(8,128)} copy(f32[3,3,8,128]{3,2,1,0:T(8,128)S(1)} %get-tuple-element.5) | data formatting | bytes 73728
